TPU v7x, 512 devices: a whole 4x4x16 slice. The times are simulated.
512 devices in a mesh: dp: 16 (over z), cell: 32 (over y, x, core).
Axes of the slice: x: 4, y: 4, z: 16, core: 2. Of those that a mesh axis runs over, the one named last changes fastest.
Arguments:
- counts: bfloat16 [16, 2048, 32768], P('dp', None, 'cell'), may hold values from 1 to 50
- shared: float32 [32, 2048], replicated, may hold values from 0.2 to 1.2
- view_factors: float32 [16, 32, 2048], P('dp'), may hold values from 0.2 to 1.2
- loadings: float32 [16, 32, 32768], P('dp', None, 'cell'), may hold values from 0.1 to 1
Outputs:
- shared_out: float32 [32, 2048], replicated
- views_out: float32 [16, 32, 2048], P('dp')
- loadings_out: float32 [16, 32, 32768], P('dp', None, 'cell')
All inputs are finite; a program needn't handle non-finite values.
Results may differ from a plain program's by a relative error of at most 0.0004.
Values sent between devices are 32-bit elements; how exact they have to be, the bound alone decides.
A program may use at most 64 MiB of HBM per device.

v0:
```python
import jax
import jax.numpy as jnp
from jax import lax
from jax.sharding import PartitionSpec as P

ITERS = 3
OUTER_STEPS = 2


penalty = 5.0


def highest(left, right):
    return jnp.dot(left, right, precision=lax.Precision.HIGHEST, preferred_element_type=jnp.float32)


def local(counts, shared, view_factors, loadings):
    matrix = counts[0]
    view_factor = view_factors[0]
    loading = loadings[0]
    for sweep_index in range(OUTER_STEPS):
        for inner_index in range(ITERS):
            combined = shared + view_factor
            numerator = jnp.dot(
                combined.astype(jnp.bfloat16), matrix, preferred_element_type=jnp.float32
            )
            gramian = highest(combined, combined.T) + penalty * highest(view_factor, view_factor.T)
            loading = loading * numerator / highest(gramian, loading)
            rounded = loading.astype(jnp.bfloat16)
            partial_value = lax.dot_general(
                rounded, matrix, (((1,), (1,)), ((), ())), preferred_element_type=jnp.float32
            )
            square_part = highest(loading, loading.T)
            crossed, squared = lax.psum((partial_value, square_part), "cell")
            view_factor = view_factor * crossed / highest(squared, combined + penalty * view_factor)
        denominator = highest(squared, shared + view_factor)
        totals, denominator_all = lax.psum((crossed, denominator), "dp")
        shared = shared * totals / denominator_all
    return (shared, view_factor[None], loading[None])


def solution(mesh):
    in_specs = (P("dp", None, "cell"), P(), P("dp", None, None), P("dp", None, "cell"))
    out_specs = (P(), P("dp", None, None), P("dp", None, "cell"))
    return jax.shard_map(local, mesh=mesh, in_specs=in_specs, out_specs=out_specs, check_vma=False)
```

profile of v0, /device:TPU:1, one launch (start us, length us, event | category | flops | bytes accessed | tf_op | source)
XLA Modules:
  0.0 1128.1 jit_solution(17119749460146105586)
XLA Ops:
  7.2 1.7 fusion.109
  8.9 1.4 fusion.65
  10.3 1.2 fusion.83
  11.5 3.2 fusion.27
  14.8 2.0 fusion.20
  17.1 125.0 %psum.113 = f32[32,32]{1,0:T(8,128)S(1)} all-reduce(f32[32,32]{1,0:T(8,128)S(1)} %fusion.130), channel_id=1, replica_groups=mesh['dp'=16,'cell'=32] {'cell'}, use_global_device_ids=true, to_apply=%region_1.0 | all-reduce | flops 1024 | bytes 8192 | tf_op jit(solution)/shard_map/psum | solution.py:34
  142.2 12.1 %all-reduce.11.cloned.1.call-done = f32[32,2048]{1,0:T(8,128)} async-done(((f32[32,2048]{1,0:T(8,128)}), f32[32,2048]{1,0:T(8,128)}) %all-reduce.11.cloned.1.call-update) | async-done | bytes 262160 | tf_op jit(solution)/shard_map/psum | solution.py:34
  154.3 1.5 convolution_divide_fusion.5
  155.7 0.4 fusion.127
  156.1 0.4 fusion.64
  156.7 3.0 fusion.33
  159.7 2.0 fusion.16
  162.1 122.2 %psum.115 = f32[32,32]{1,0:T(8,128)S(1)} all-reduce(f32[32,32]{1,0:T(8,128)S(1)} %fusion.132), channel_id=1, replica_groups=mesh['dp'=16,'cell'=32] {'cell'}, use_global_device_ids=true, to_apply=%region_3.0 | all-reduce | flops 1024 | bytes 8192 | tf_op jit(solution)/shard_map/psum | solution.py:34
  284.3 9.6 all-reduce.13.cloned.1.call-done
  293.9 1.5 convolution_divide_fusion.4
  295.3 0.4 fusion.123
  296.3 3.0 fusion.39
  299.4 2.0 fusion.12
  301.7 122.2 %psum.118 = f32[32,32]{1,0:T(8,128)S(1)} all-reduce(f32[32,32]{1,0:T(8,128)S(1)} %fusion.134), channel_id=1, replica_groups=mesh['dp'=16,'cell'=32] {'cell'}, use_global_device_ids=true, to_apply=%region_6.0 | all-reduce | flops 1024 | bytes 8192 | tf_op jit(solution)/shard_map/psum | solution.py:34
  423.9 9.6 all-reduce.15.cloned.1.call-done
  433.6 1.3 convolution_divide_fusion.3
  434.9 1.1 fusion.77
  436.0 127.9 %all-reduce.25.cloned.1.call-done = (f32[32,2048]{1,0:T(8,128)}, f32[32,2048]{1,0:T(8,128)}) async-done(((f32[32,2048]{1,0:T(8,128)}, f32[32,2048]{1,0:T(8,128)}), (f32[32,2048]{1,0:T(8,128)}, f32[32,2048]{1,0:T(8,128)})) %all-reduce.25.cloned.1.call-update) | async-done | bytes 524304 | tf_op jit(solution)/shard_map/psum | solution.py:37
  563.9 1.2 multiply_divide_fusion.1
  565.1 0.4 fusion.119
  565.5 0.4 fusion.62
  566.1 3.0 fusion.45
  569.2 2.0 fusion.8
  571.5 128.6 %psum.121 = f32[32,32]{1,0:T(8,128)S(1)} all-reduce(f32[32,32]{1,0:T(8,128)S(1)} %fusion.136), channel_id=1, replica_groups=mesh['dp'=16,'cell'=32] {'cell'}, use_global_device_ids=true, to_apply=%region_9.0 | all-reduce | flops 1024 | bytes 8192 | tf_op jit(solution)/shard_map/psum | solution.py:34
  700.1 9.5 all-reduce.17.cloned.1.call-done
  709.6 1.5 convolution_divide_fusion.2
  711.1 0.4 fusion.115
  711.5 0.4 fusion.61
  712.1 3.0 fusion.51
  715.1 2.0 fusion.4
  717.5 122.2 %psum.123 = f32[32,32]{1,0:T(8,128)S(1)} all-reduce(f32[32,32]{1,0:T(8,128)S(1)} %fusion.138), channel_id=1, replica_groups=mesh['dp'=16,'cell'=32] {'cell'}, use_global_device_ids=true, to_apply=%region_11.0 | all-reduce | flops 1024 | bytes 8192 | tf_op jit(solution)/shard_map/psum | solution.py:34
  839.7 9.7 all-reduce.19.cloned.1.call-done
  849.3 1.5 convolution_divide_fusion.1
  850.8 0.4 fusion.111
  851.2 0.4 fusion.60
  851.8 3.0 fusion.57
  854.8 2.0 fusion
  857.2 122.2 %psum.126 = f32[32,32]{1,0:T(8,128)S(1)} all-reduce(f32[32,32]{1,0:T(8,128)S(1)} %fusion.140), channel_id=1, replica_groups=mesh['dp'=16,'cell'=32] {'cell'}, use_global_device_ids=true, to_apply=%region_14.0 | all-reduce | flops 1024 | bytes 8192 | tf_op jit(solution)/shard_map/psum | solution.py:34
  979.4 9.6 all-reduce.21.cloned.1.call-done
  989.0 1.3 convolution_divide_fusion
  990.3 1.1 fusion.69
  991.4 128.1 %all-reduce.23.cloned.1.call-done = (f32[32,2048]{1,0:T(8,128)}, f32[32,2048]{1,0:T(8,128)}) async-done(((f32[32,2048]{1,0:T(8,128)}, f32[32,2048]{1,0:T(8,128)}), (f32[32,2048]{1,0:T(8,128)}, f32[32,2048]{1,0:T(8,128)})) %all-reduce.23.cloned.1.call-update) | async-done | bytes 524304 | tf_op jit(solution)/shard_map/psum | solution.py:37
  1119.5 1.8 multiply_divide_fusion
  (48 shorter events, 3.6 us)
Async XLA Ops:
  7.2 147.1 %all-reduce.11.cloned.1.call-start = ((), (), s32[]{:S(2)}) async-start(), calls=%async_computation | async-start | bytes 524288 | tf_op jit(solution)/shard_map/psum | solution.py:34
  7.2 7.5 copy-start
  11.5 142.8 %copy-start.6 = (f32[32,2048]{1,0:T(8,128)S(1)}, f32[32,2048]{1,0:T(8,128)}, u32[]{:S(2)}) copy-start(f32[32,2048]{1,0:T(8,128)} %param.5) | copy-start | bytes 786436
  11.5 142.8 %copy-start.7 = (f32[1,32,2048]{2,1,0:T(8,128)S(1)}, f32[1,32,2048]{2,1,0:T(8,128)}, u32[]{:S(2)}) copy-start(f32[1,32,2048]{2,1,0:T(8,128)} %param.6) | copy-start | bytes 786436
  16.8 277.1 %all-reduce.13.cloned.1.call-start = ((), (), s32[]{:S(2)}) async-start(), calls=%async_computation.1 | async-start | bytes 524288 | tf_op jit(solution)/shard_map/psum | solution.py:34
  154.3 5.5 copy-start.1
  161.8 271.8 %all-reduce.15.cloned.1.call-start = ((), (), s32[]{:S(2)}) async-start(), calls=%async_computation.2 | async-start | bytes 524288 | tf_op jit(solution)/shard_map/psum | solution.py:34
  293.9 5.5 copy-start.2
  301.4 262.5 %all-reduce.25.cloned.1.call-start = ((), (), s32[]{:S(2)}) async-start(), calls=%async_computation.7 | async-start | bytes 1048576 | tf_op jit(solution)/shard_map/psum | solution.py:37
  436.0 273.7 %all-reduce.17.cloned.1.call-start = ((), (), s32[]{:S(2)}) async-start(), calls=%async_computation.3 | async-start | bytes 524288 | tf_op jit(solution)/shard_map/psum | solution.py:34
  563.9 5.2 copy-start.3
  571.2 278.1 %all-reduce.19.cloned.1.call-start = ((), (), s32[]{:S(2)}) async-start(), calls=%async_computation.4 | async-start | bytes 524288 | tf_op jit(solution)/shard_map/psum | solution.py:34
  709.6 5.5 copy-start.4
  717.2 271.8 %all-reduce.21.cloned.1.call-start = ((), (), s32[]{:S(2)}) async-start(), calls=%async_computation.5 | async-start | bytes 524288 | tf_op jit(solution)/shard_map/psum | solution.py:34
  849.3 5.5 copy-start.5
  854.8 266.4 %copy-start.8 = (f32[32,1024]{1,0:T(8,128)}, f32[32,1024]{1,0:T(8,128)S(1)}, u32[]{:S(2)}) copy-start(f32[32,1024]{1,0:T(8,128)S(1)} %fusion.57) | copy-start | bytes 393220
  856.9 262.6 %all-reduce.23.cloned.1.call-start = ((), (), s32[]{:S(2)}) async-start(), calls=%async_computation.6 | async-start | bytes 1048576 | tf_op jit(solution)/shard_map/psum | solution.py:37
  990.3 130.9 %copy-start.9 = (f32[32,2048]{1,0:T(8,128)}, f32[32,2048]{1,0:T(8,128)S(1)}, u32[]{:S(2)}) copy-start(f32[32,2048]{1,0:T(8,128)S(1)} %convolution_divide_fusion) | copy-start | bytes 786436
Sparse Core Ops, SparseCore 0:
  16.9 137.2 all-reduce.10
  161.9 131.8 all-reduce.12
  301.6 131.9 all-reduce.14
  436.5 127.3 all-reduce.24
  571.3 138.2 all-reduce.16
  717.3 131.9 all-reduce.18
  857.0 131.9 all-reduce.20
  992.0 127.3 all-reduce.22
where the time goes:
time: 1140 us; the launch traced here: 1130 us
  blocking collectives  742 us (65%)
  waiting for transfers between devices  316 us (28%)
  matrix products  51.6 us (5%)
  between operations  14.6 us (1%)
    psum x6, blocking collectives, local(): crossed, squared = lax.psum((partial_value, square_part), 'cell')  742 us
    psum x2, waiting for transfers between devices, local(): totals, denominator_all = lax.psum((crossed, denominator), 'dp')  256 us
    psum x6, waiting for transfers between devices, local(): crossed, squared = lax.psum((partial_value, square_part), 'cell')  60.1 us
  transfers between devices with their start and end apart: 8, of which 8 were waited for; matrix products, arithmetic and copies ran while one was open for 0% of the time, Pallas kernels for 0%

commit v1 on v0

v1 whole, which is shorter than its diff:
```python
import functools

import jax
import jax.numpy as jnp
from jax import lax
from jax.experimental import pallas as pl
from jax.experimental.pallas import tpu as pltpu
from jax.sharding import PartitionSpec as P

ITERS = 3
OUTER_STEPS = 2
PENALTY = 5.0

SIDE = 4
CHIPS = SIDE * SIDE
DEVICES = 2 * CHIPS
SETS = 16
RANK = 32
LANES = 128
ROWS = RANK // 2
HALF = ROWS // 2

f32, bf16 = jnp.float32, jnp.bfloat16
MESH = pl.DeviceIdType.MESH
NN = (((1,), (0,)), ((), ()))
NT = (((1,), (1,)), ((), ()))


def hops(d):
    return min(d, SIDE - d)


OFFSETS = sorted(
    ((dy, dx) for dy in range(SIDE) for dx in range(SIDE)),
    key=lambda o: (hops(o[0]) + hops(o[1]), o),
)
DISTANCE = [hops(dy) + hops(dx) for dy, dx in OFFSETS]
GROUPS = 5
GROUP_SIZE = [2 * DISTANCE.count(g) for g in range(GROUPS)]
GROUP_SIZE[0] = 1


def dot(a, b, dims=NN):
    return lax.dot_general(a, b, dims, preferred_element_type=f32)


def split(v):
    high = v.astype(bf16)
    return high, (v - high.astype(f32)).astype(bf16)


def kernel(
    x_hbm, w_hbm, v_hbm, h_hbm, w_out, v_out, h_out,
    x, w, v, h, n, z, parts, qsrc, pslots, qslots, m4, psum, qsum,
    zsrc, zpair, zhalf, zslots, wold,
    xsem, insem, outsem, psend, precv, qsend, qrecv, vsend, vrecv,
    z1send, z1recv, z2send, z2recv, z3send, z3recv, wsend, wrecv,
):
    dp = lax.axis_index("dp")
    me = lax.axis_index("cell")
    core = lax.rem(me, 2)
    chip = lax.div(me, 2)
    cy, cx = lax.div(chip, SIDE), lax.rem(chip, SIDE)
    parity = lax.rem(dp, 2)
    pair = dp + 1 - 2 * parity
    chips = [lax.rem(cy + dy, SIDE) * SIDE + lax.rem(cx + dx, SIDE) for dy, dx in OFFSETS]
    zothers = [lax.rem(dp + 2 * s, SETS) for s in range(1, SETS // 2)]

    def partners(i):
        if i == 0:
            return [(chip, 1 - core)]
        return [(chips[i], core), (chips[i], 1 - core)]

    def remote(src, dst, send, recv, where):
        return pltpu.make_async_remote_copy(
            src_ref=src, dst_ref=dst, send_sem=send, recv_sem=recv,
            device_id=where, device_id_type=MESH,
        )

    def settle(ref, send, recv):
        return remote(ref, ref, send, recv, {"cell": chip * 2 + 1 - core})

    barrier = pltpu.get_barrier_semaphore()
    count = 0
    for i in range(CHIPS):
        for c, k in partners(i):
            pl.semaphore_signal(barrier, inc=1, device_id={"cell": c * 2 + k}, device_id_type=MESH)
            count += 1
    for other in [pair] + zothers:
        pl.semaphore_signal(barrier, inc=1, device_id={"dp": other}, device_id_type=MESH)
        count += 1

    def load_h():
        return pltpu.make_async_copy(h_hbm, h, insem.at[2])

    def load_x(i):
        rows = pl.ds(pl.multiple_of(chips[i] * LANES, LANES), LANES)
        return pltpu.make_async_copy(x_hbm.at[rows], x.at[rows], xsem.at[i])

    def load_f(src, dst, c, s):
        return pltpu.make_async_copy(src.at[:, pl.ds(c * LANES, LANES)], dst.at[c], insem.at[s])

    for c in range(CHIPS):
        load_f(w_hbm, w, c, 0).start()
        load_f(v_hbm, v, c, 1).start()
    load_h().start()
    for i in range(CHIPS):
        load_x(i).start()
    pltpu.make_async_copy(w, w, insem.at[0]).wait()
    pltpu.make_async_copy(v, v, insem.at[1]).wait()

    def gather(i, c, first):
        vc = v[c]
        a = w[c] + vc
        ah, al = split(a)
        vh, vl = split(vc)
        s = jnp.concatenate([ah, al, vh, vl], axis=0)
        rows = pl.ds(pl.multiple_of(c * LANES, LANES), LANES)
        dn, dz = dot(ah, x[rows, :]), dot(s, s, NT)
        if first:
            n[...] = dn
            z[...] = dz
        else:
            n[...] += dn
            z[...] += dz

    for i in range(CHIPS):
        load_x(i).wait()
        gather(i, chips[i], i == 0)
    load_h().wait()
    pl.semaphore_wait(barrier, count)

    lane = lax.broadcasted_iota(jnp.int32, (RANK, LANES), 1)
    block = lane // RANK
    mine = pl.ds(pl.multiple_of(core * ROWS, ROWS), ROWS)

    def spread(m):
        high, low = split(m)
        return jnp.concatenate([jnp.concatenate([high, low], axis=1)] * 4, axis=0)

    def square_times(packed, right):
        both = jnp.concatenate([packed, packed], axis=0)
        row = lax.broadcasted_iota(jnp.int32, (ROWS, LANES), 0)
        keep = block[:ROWS] == 2 * core + row // 8
        high, low = split(jnp.where(keep, both, 0.0))
        r = dot(jnp.concatenate([high, low], axis=0), right)
        return (r[:ROWS, :LANES] + r[ROWS:, :LANES]) + (r[:ROWS, LANES:] + r[ROWS:, LANES:])

    def step(t, carry):
        zz = z[...]
        y = jnp.where(lane < 64, zz[:32] + zz[32:64], PENALTY * (zz[64:96] + zz[96:]))
        y = y + pltpu.roll(y, 64, 1)
        y = y + pltpu.roll(y, 32, 1)
        gh, gl = split(y)
        left = jnp.where(lane < 64, gh.astype(f32), gl.astype(f32)).astype(bf16)
        hv = h[...]
        hh, hl = split(hv)
        hv = hv * n[...] / dot(left, jnp.concatenate([hh, hl, hh, hl], axis=0))
        h[...] = hv
        hh, hl = split(hv)

        two = jnp.concatenate([hh, hl], axis=0)
        q = dot(two, jnp.concatenate([two, two], axis=0), NT)
        q = q[:32] + q[32:]
        q = q + pltpu.roll(q, 32, 1)
        q = jnp.where(block == lax.broadcasted_iota(jnp.int32, (RANK, LANES), 0) // 8, q, 0.0)
        packed = (q[0:8] + q[8:16]) + (q[16:24] + q[24:32])
        qsrc[...] = packed
        qslots[me] = packed
        for i in reversed(range(CHIPS)):
            for c, k in partners(i):
                remote(qsrc, qslots.at[me], qsend, qrecv, {"cell": c * 2 + k}).start()

        old = v[chip]
        shared = w[chip]
        wold[...] = shared
        m4[...] = spread(shared + old + PENALTY * old)

        for i in reversed(range(CHIPS)):
            c = chips[i]
            rows = pl.ds(pl.multiple_of(c * LANES, LANES), LANES)
            parts[c] = dot(hh, x[rows, :], NT)
            for c, k in partners(i):
                its = pl.ds(pl.multiple_of(k * ROWS, ROWS), ROWS)
                remote(parts.at[c, its], pslots.at[me], psend, precv, {"cell": c * 2 + k}).start()
        pslots[me] = parts[chip, mine]

        settle(qslots.at[pl.ds(0, DEVICES - 1)], qsend, qrecv).wait()
        qt = qslots[0]
        for i in range(1, DEVICES):
            qt = qt + qslots[i]
        qsum[...] = qt
        d = square_times(qt, m4[...])
        settle(pslots.at[pl.ds(0, DEVICES - 1)], psend, precv).wait()
        pt = pslots[0]
        for i in range(1, DEVICES):
            pt = pt + pslots[i]
        psum[...] = pt
        v[chip, mine] = v[chip, mine] * pt / d
        for i in reversed(range(CHIPS)):
            for c, k in partners(i):
                piece = v.at[chip, mine]
                remote(piece, piece, vsend, vrecv.at[DISTANCE[i]], {"cell": c * 2 + k}).start()

        def wait_v(g):
            settle(pslots.at[pl.ds(0, GROUP_SIZE[g])], vsend, vrecv.at[g]).wait_recv()

        wait_v(0)

        @pl.when(lax.rem(t, ITERS) == ITERS - 1)
        def _():
            d = square_times(qsum[...], spread(wold[...] + v[chip]))
            turn = lax.div(t, ITERS)
            for p in range(2):
                eight = pl.ds(p * HALF, HALF)
                zsrc[p, 0] = psum[eight, :]
                zsrc[p, 1] = d[p * HALF : (p + 1) * HALF]
            first = remote(zsrc.at[1 - parity], zpair, z1send, z1recv, {"dp": pair})
            first.start()
            first.wait()
            half = zsrc[parity] + zpair[...]
            zhalf[...] = half
            spot = lax.div(dp, 2)
            zslots[turn, spot] = half
            for other in zothers:
                remote(
                    zhalf, zslots.at[turn, spot], z2send.at[turn], z2recv.at[turn], {"dp": other}
                ).start()
            settle(zslots.at[turn, pl.ds(0, SETS // 2 - 1)], z2send.at[turn], z2recv.at[turn]).wait()
            total = zslots[turn, 0]
            for i in range(1, SETS // 2):
                total = total + zslots[turn, i]
            ours = pl.ds(pl.multiple_of(core * ROWS + parity * HALF, HALF), HALF)
            w[chip, ours] = w[chip, ours] * total[0] / total[1]
            piece = w.at[chip, ours]
            back = remote(piece, piece, z3send, z3recv, {"dp": pair})
            back.start()
            back.wait()
            for i in reversed(range(CHIPS)):
                for c, k in partners(i):
                    piece = w.at[chip, mine]
                    remote(piece, piece, wsend, wrecv, {"cell": c * 2 + k}).start()
            settle(pslots.at[pl.ds(0, DEVICES - 1)], wsend, wrecv).wait()

        @pl.when(t < ITERS * OUTER_STEPS - 1)
        def _():
            for i in range(CHIPS):
                if i and DISTANCE[i] != DISTANCE[i - 1]:
                    wait_v(DISTANCE[i])
                gather(i, chips[i], i == 0)

        @pl.when(t == ITERS * OUTER_STEPS - 1)
        def _():
            for g in range(1, GROUPS):
                wait_v(g)

        settle(pslots.at[pl.ds(0, DEVICES - 1)], vsend, vrecv.at[0]).wait_send()
        return carry

    lax.fori_loop(0, ITERS * OUTER_STEPS, step, 0)

    pltpu.make_async_copy(h, h_out, outsem.at[0]).start()
    for c in range(CHIPS):
        pltpu.make_async_copy(v.at[c], v_out.at[:, pl.ds(c * LANES, LANES)], outsem.at[1]).start()
        pltpu.make_async_copy(w.at[c], w_out.at[:, pl.ds(c * LANES, LANES)], outsem.at[2]).start()
    pltpu.make_async_copy(h, h_out, outsem.at[0]).wait()
    pltpu.make_async_copy(v, v, outsem.at[1]).wait()
    pltpu.make_async_copy(w, w, outsem.at[2]).wait()


def local(counts, shared, view_factors, loadings):
    genes, cells = counts.shape[1:]
    vmem = functools.partial(pltpu.VMEM, dtype=f32)
    dma = pltpu.SemaphoreType.DMA
    hbm = pl.BlockSpec(memory_space=pl.ANY)
    w, v, h = pl.pallas_call(
        kernel,
        out_shape=[
            jax.ShapeDtypeStruct((RANK, genes), f32),
            jax.ShapeDtypeStruct((RANK, genes), f32),
            jax.ShapeDtypeStruct((RANK, cells), f32),
        ],
        in_specs=[hbm] * 4,
        out_specs=[hbm] * 3,
        scratch_shapes=[
            pltpu.VMEM((genes, cells), bf16),
            vmem((CHIPS, RANK, LANES)),
            vmem((CHIPS, RANK, LANES)),
            vmem((RANK, cells)),
            vmem((RANK, cells)),
            vmem((LANES, LANES)),
            vmem((CHIPS, RANK, LANES)),
            vmem((8, LANES)),
            vmem((DEVICES, ROWS, LANES)),
            vmem((DEVICES, 8, LANES)),
            pltpu.VMEM((LANES, 2 * LANES), bf16),
            vmem((ROWS, LANES)),
            vmem((8, LANES)),
            vmem((2, 2, HALF, LANES)),
            vmem((2, HALF, LANES)),
            vmem((2, HALF, LANES)),
            vmem((OUTER_STEPS, SETS // 2, 2, HALF, LANES)),
            vmem((RANK, LANES)),
            dma((CHIPS,)), dma((3,)), dma((3,)),
            dma, dma, dma, dma, dma, dma((GROUPS,)),
            dma, dma, dma((OUTER_STEPS,)), dma((OUTER_STEPS,)), dma, dma, dma, dma,
        ],
        compiler_params=pltpu.CompilerParams(
            collective_id=0, has_side_effects=True, vmem_limit_bytes=40 * 2**20
        ),
    )(counts[0], shared, view_factors[0], loadings[0])
    return w, v[None], h[None]


def solution(mesh):
    in_specs = (P("dp", None, "cell"), P(), P("dp", None, None), P("dp", None, "cell"))
    out_specs = (P(), P("dp", None, None), P("dp", None, "cell"))
    return jax.shard_map(local, mesh=mesh, in_specs=in_specs, out_specs=out_specs, check_vma=False)
```

time: 1140 us -> 142 us (0.12)
  blocking collectives: 742 us -> 0 us
  waiting for transfers between devices: 316 us -> 0 us
  Pallas kernels: 0 us -> 134 us
  matrix products: 51.6 us -> 0 us
  between operations: 14.6 us -> 0.65 us
    psum x6 -> x0, blocking collectives: 742 us -> none  [local(): crossed, squared = lax.psum((partial_value, square_part), 'cell')]
    psum x8 -> x0, waiting for transfers between devices: 316 us -> none  [the longest x2 256 us: local(): totals, denominator_all = lax.psum((crossed, denominator), 'dp')]
    pallas_call x0 -> x1, Pallas kernels: none -> 134 us  [local(): pl.pallas_call(kernel, out_shape=[jax.ShapeDtypeStruct((RANK, genes), f32...]
    dot_general x44 -> x0, matrix products: 51.6 us -> none  [the longest x32 21 us: highest(): jnp.dot(left, right, precision=lax.Precision.HIGHEST, preferred_element_t...]
  transfers between devices with their start and end apart: 8 -> 0, of which waited for: 8 -> 0; matrix products, arithmetic and copies ran while one was open for 0% -> 0% of each run, Pallas kernels for 0% -> 0%
where the time goes in v1:
time: 142 us; the launch traced here: 141 us
  Pallas kernels  134 us (94%)
  local copies, waits for them, and re-layouts  7.05 us (5%)
    pallas_call x1, Pallas kernels, local(): pl.pallas_call(kernel, out_shape=[jax.ShapeDtypeStruct((RANK, genes), f32...  134 us
    unnamed x11, local copies, waits for them, and re-layouts  7.05 us

profile of v1, /device:TPU:1, one launch (start us, length us, event | category | flops | bytes accessed | tf_op | source)
XLA Modules:
  0.0 141.3 jit_solution(1890117568198778179)
XLA Ops:
  0.6 0.0 copy-start
  0.6 2.2 %copy-done = bf16[1,2048,1024]{2,1,0:T(8,128)(2,1)S(1)} copy-done((bf16[1,2048,1024]{2,1,0:T(8,128)(2,1)S(1)}, bf16[1,2048,1024]{2,1,0:T(8,128)(2,1)}, u32[]{:S(2)}) %copy-start) | copy-done | bytes 4194328
  2.8 0.0 copy-start.1
  2.8 0.9 copy-done.1
  3.8 0.0 copy-start.2
  3.8 0.9 copy-done.2
  4.7 0.0 copy-start.3
  4.7 0.9 copy-done.3
  5.6 133.6 %shard_map.67 = (f32[32,2048]{1,0:T(8,128)S(1)}, f32[32,2048]{1,0:T(8,128)S(1)}, f32[32,1024]{1,0:T(8,128)S(1)}) custom-call(bf16[2048,1024]{1,0:T(8,128)(2,1)S(1)} %bitcast.5, f32[32,2048]{1,0:T(8,128)S(1)} %copy-done.1, f32[32,2048]{1,0:T(8,128)S(1)} %bitcast.6, f32[32,1024]{1,0:T(8,128)S(1)} %bitcast.8), custom_call_target="tpu_custom_call" | custom-call | tf_op jit(solution)/shard_map/pallas_call | solution.py:276
  139.2 0.7 copy.10
  140.0 0.7 copy.11
  140.7 0.7 copy.12
Async XLA Ops:
  0.6 2.2 %copy-start = (bf16[1,2048,1024]{2,1,0:T(8,128)(2,1)S(1)}, bf16[1,2048,1024]{2,1,0:T(8,128)(2,1)}, u32[]{:S(2)}) copy-start(bf16[1,2048,1024]{2,1,0:T(8,128)(2,1)} %param.4) | copy-start | bytes 12582916
  2.8 0.9 copy-start.1
  3.8 0.9 copy-start.2
  4.7 0.9 copy-start.3

commit v2 on v1

--- a/solution.py
+++ b/solution.py
@@ -34,10 +34,7 @@
     ((dy, dx) for dy in range(SIDE) for dx in range(SIDE)),
     key=lambda o: (hops(o[0]) + hops(o[1]), o),
 )
-DISTANCE = [hops(dy) + hops(dx) for dy, dx in OFFSETS]
-GROUPS = 5
-GROUP_SIZE = [2 * DISTANCE.count(g) for g in range(GROUPS)]
-GROUP_SIZE[0] = 1
+MIRROR = [OFFSETS.index((-dy % SIDE, -dx % SIDE)) for dy, dx in OFFSETS]
 
 
 def dot(a, b, dims=NN):
@@ -51,10 +48,10 @@
 
 def kernel(
     x_hbm, w_hbm, v_hbm, h_hbm, w_out, v_out, h_out,
-    x, w, v, h, n, z, parts, qsrc, pslots, qslots, m4, psum, qsum,
-    zsrc, zpair, zhalf, zslots, wold,
+    x, w, v, h, n, z, parts, qsrc, pslots, qslots, m4, qleft, wold,
+    zsrc, zpair, zhalf, zslots, blank,
     xsem, insem, outsem, psend, precv, qsend, qrecv, vsend, vrecv,
-    z1send, z1recv, z2send, z2recv, z3send, z3recv, wsend, wrecv,
+    z1send, z1recv, z2send, z2recv, wsend, wrecv, hand,
 ):
     dp = lax.axis_index("dp")
     me = lax.axis_index("cell")
@@ -64,7 +61,10 @@
     parity = lax.rem(dp, 2)
     pair = dp + 1 - 2 * parity
     chips = [lax.rem(cy + dy, SIDE) * SIDE + lax.rem(cx + dx, SIDE) for dy, dx in OFFSETS]
-    zothers = [lax.rem(dp + 2 * s, SETS) for s in range(1, SETS // 2)]
+    zothers = [lax.rem(dp + 2 * s, SETS) for s in (4, 3, 5, 2, 6, 1, 7)]
+
+    def along(s):
+        return {"dp": lax.rem(dp + s + SETS, SETS)}
 
     def partners(i):
         if i == 0:
@@ -86,8 +86,8 @@
         for c, k in partners(i):
             pl.semaphore_signal(barrier, inc=1, device_id={"cell": c * 2 + k}, device_id_type=MESH)
             count += 1
-    for other in [pair] + zothers:
-        pl.semaphore_signal(barrier, inc=1, device_id={"dp": other}, device_id_type=MESH)
+    for s in (-2, -1, 1, 2):
+        pl.semaphore_signal(barrier, inc=1, device_id=along(s), device_id_type=MESH)
         count += 1
 
     def load_h():
@@ -130,7 +130,11 @@
     load_h().wait()
     pl.semaphore_wait(barrier, count)
 
+    for where in (along(-2), along(2), {"dp": pair}):
+        pl.semaphore_signal(hand.at[0], inc=1, device_id=where, device_id_type=MESH)
+
     lane = lax.broadcasted_iota(jnp.int32, (RANK, LANES), 1)
+    row = lax.broadcasted_iota(jnp.int32, (RANK, LANES), 0)
     block = lane // RANK
     mine = pl.ds(pl.multiple_of(core * ROWS, ROWS), ROWS)
 
@@ -138,13 +142,19 @@
         high, low = split(m)
         return jnp.concatenate([jnp.concatenate([high, low], axis=1)] * 4, axis=0)
 
-    def square_times(packed, right):
-        both = jnp.concatenate([packed, packed], axis=0)
-        row = lax.broadcasted_iota(jnp.int32, (ROWS, LANES), 0)
-        keep = block[:ROWS] == 2 * core + row // 8
-        high, low = split(jnp.where(keep, both, 0.0))
-        r = dot(jnp.concatenate([high, low], axis=0), right)
+    def square_times(left, right):
+        r = dot(left, right)
         return (r[:ROWS, :LANES] + r[ROWS:, :LANES]) + (r[:ROWS, LANES:] + r[ROWS:, LANES:])
+
+    def to_all(piece, send, recvs):
+        for other in (1, 0):
+            for i in reversed(range(CHIPS)):
+                if other or i:
+                    k = 1 - core if other else core
+                    remote(piece, piece, send, recvs.at[MIRROR[i]], {"cell": chips[i] * 2 + k}).start()
+
+    def wait_v(i):
+        settle(pslots.at[pl.ds(0, 2 if i else 1)], vsend, vrecv.at[i]).wait_recv()
 
     def step(t, carry):
         zz = z[...]
@@ -163,13 +173,15 @@
         q = dot(two, jnp.concatenate([two, two], axis=0), NT)
         q = q[:32] + q[32:]
         q = q + pltpu.roll(q, 32, 1)
-        q = jnp.where(block == lax.broadcasted_iota(jnp.int32, (RANK, LANES), 0) // 8, q, 0.0)
-        packed = (q[0:8] + q[8:16]) + (q[16:24] + q[24:32])
-        qsrc[...] = packed
-        qslots[me] = packed
+        q = jnp.where(block == lax.rem(row // 4, 4), q, 0.0)
+        for k in range(2):
+            packed = q[ROWS * k : ROWS * k + 8] + q[ROWS * k + 8 : ROWS * k + 16]
+            packed = packed + pltpu.roll(packed, 4, 0)
+            qsrc[k] = packed[:4]
+        qslots[me] = qsrc[core]
         for i in reversed(range(CHIPS)):
             for c, k in partners(i):
-                remote(qsrc, qslots.at[me], qsend, qrecv, {"cell": c * 2 + k}).start()
+                remote(qsrc.at[k], qslots.at[me], qsend, qrecv, {"cell": c * 2 + k}).start()
 
         old = v[chip]
         shared = w[chip]
@@ -189,83 +201,116 @@
         qt = qslots[0]
         for i in range(1, DEVICES):
             qt = qt + qslots[i]
-        qsum[...] = qt
-        d = square_times(qt, m4[...])
+        qt = jnp.where(block[:ROWS] == row[:ROWS] // 4, jnp.concatenate([qt] * 4, axis=0), 0.0)
+        left = jnp.concatenate(split(qt), axis=0)
+        qleft[...] = left
+        d = square_times(left, m4[...])
         settle(pslots.at[pl.ds(0, DEVICES - 1)], psend, precv).wait()
         pt = pslots[0]
         for i in range(1, DEVICES):
             pt = pt + pslots[i]
-        psum[...] = pt
-        v[chip, mine] = v[chip, mine] * pt / d
-        for i in reversed(range(CHIPS)):
-            for c, k in partners(i):
-                piece = v.at[chip, mine]
-                remote(piece, piece, vsend, vrecv.at[DISTANCE[i]], {"cell": c * 2 + k}).start()
-
-        def wait_v(g):
-            settle(pslots.at[pl.ds(0, GROUP_SIZE[g])], vsend, vrecv.at[g]).wait_recv()
-
-        wait_v(0)
-
-        @pl.when(lax.rem(t, ITERS) == ITERS - 1)
+        turn = lax.div(t, ITERS)
+        last = lax.rem(t, ITERS) == ITERS - 1
+
+        @pl.when(t == 0)
         def _():
-            d = square_times(qsum[...], spread(wold[...] + v[chip]))
-            turn = lax.div(t, ITERS)
-            for p in range(2):
-                eight = pl.ds(p * HALF, HALF)
-                zsrc[p, 0] = psum[eight, :]
-                zsrc[p, 1] = d[p * HALF : (p + 1) * HALF]
-            first = remote(zsrc.at[1 - parity], zpair, z1send, z1recv, {"dp": pair})
-            first.start()
-            first.wait()
-            half = zsrc[parity] + zpair[...]
-            zhalf[...] = half
+            pl.semaphore_wait(hand.at[0], 3)
+            for s in (-4, 4):
+                pl.semaphore_signal(hand.at[1], inc=1, device_id=along(s), device_id_type=MESH)
+
+        def to_pair(j):
+            return remote(zsrc.at[j, 1 - parity], zpair.at[j], z1send.at[j], z1recv.at[j], {"dp": pair})
+
+        def halve(j, total):
+            zsrc[j, 0] = total[:HALF]
+            zsrc[j, 1] = total[HALF:]
+            to_pair(j).start()
+
+        def to_others(j):
+            to_pair(j).wait()
+            half = zsrc[j, parity] + zpair[j]
+            zhalf[j] = half
             spot = lax.div(dp, 2)
-            zslots[turn, spot] = half
+            zslots[turn, j, spot] = half
             for other in zothers:
                 remote(
-                    zhalf, zslots.at[turn, spot], z2send.at[turn], z2recv.at[turn], {"dp": other}
+                    zhalf.at[j], zslots.at[turn, j, spot], z2send.at[turn, j], z2recv.at[turn, j], {"dp": other}
                 ).start()
-            settle(zslots.at[turn, pl.ds(0, SETS // 2 - 1)], z2send.at[turn], z2recv.at[turn]).wait()
-            total = zslots[turn, 0]
+
+        def over_sets(j):
+            settle(blank.at[pl.ds(0, SETS // 2 - 1)], z2send.at[turn, j], z2recv.at[turn, j]).wait()
+            total = zslots[turn, j, 0]
             for i in range(1, SETS // 2):
-                total = total + zslots[turn, i]
+                total = total + zslots[turn, j, i]
+            return total
+
+        @pl.when(last)
+        def _():
+            halve(0, pt)
+
+        v[chip, mine] = v[chip, mine] * pt / d
+        to_all(v.at[chip, mine], vsend, vrecv)
+        wait_v(0)
+
+        @pl.when(last)
+        def _():
+            halve(1, square_times(qleft[...], spread(wold[...] + v[chip])))
+
+            @pl.when(turn == 0)
+            def _():
+                pl.semaphore_wait(hand.at[1], 2)
+
+            to_others(0)
+            to_others(1)
+
+            @pl.when(turn == OUTER_STEPS - 1)
+            def _():
+                pltpu.make_async_copy(h, h_out, outsem.at[0]).start()
+                for i in range(1, CHIPS):
+                    wait_v(i)
+                for c in range(CHIPS):
+                    pltpu.make_async_copy(v.at[c], v_out.at[:, pl.ds(c * LANES, LANES)], outsem.at[1]).start()
+
+            numerator = over_sets(0)
+            denominator = over_sets(1)
             ours = pl.ds(pl.multiple_of(core * ROWS + parity * HALF, HALF), HALF)
-            w[chip, ours] = w[chip, ours] * total[0] / total[1]
+            w[chip, ours] = w[chip, ours] * numerator / denominator
             piece = w.at[chip, ours]
-            back = remote(piece, piece, z3send, z3recv, {"dp": pair})
-            back.start()
-            back.wait()
             for i in reversed(range(CHIPS)):
-                for c, k in partners(i):
-                    piece = w.at[chip, mine]
-                    remote(piece, piece, wsend, wrecv, {"cell": c * 2 + k}).start()
-            settle(pslots.at[pl.ds(0, DEVICES - 1)], wsend, wrecv).wait()
+                for z_to in (pair, dp):
+                    for k in (1 - core, core):
+                        if i or z_to is pair or k is not core:
+                            remote(piece, piece, wsend, wrecv, {"dp": z_to, "cell": chips[i] * 2 + k}).start()
+            settle(blank, wsend, wrecv).wait()
 
         @pl.when(t < ITERS * OUTER_STEPS - 1)
         def _():
             for i in range(CHIPS):
-                if i and DISTANCE[i] != DISTANCE[i - 1]:
-                    wait_v(DISTANCE[i])
+                if i:
+                    wait_v(i)
                 gather(i, chips[i], i == 0)
-
-        @pl.when(t == ITERS * OUTER_STEPS - 1)
-        def _():
-            for g in range(1, GROUPS):
-                wait_v(g)
 
         settle(pslots.at[pl.ds(0, DEVICES - 1)], vsend, vrecv.at[0]).wait_send()
         return carry
 
     lax.fori_loop(0, ITERS * OUTER_STEPS, step, 0)
 
-    pltpu.make_async_copy(h, h_out, outsem.at[0]).start()
     for c in range(CHIPS):
-        pltpu.make_async_copy(v.at[c], v_out.at[:, pl.ds(c * LANES, LANES)], outsem.at[1]).start()
         pltpu.make_async_copy(w.at[c], w_out.at[:, pl.ds(c * LANES, LANES)], outsem.at[2]).start()
     pltpu.make_async_copy(h, h_out, outsem.at[0]).wait()
     pltpu.make_async_copy(v, v, outsem.at[1]).wait()
     pltpu.make_async_copy(w, w, outsem.at[2]).wait()
+
+
+def deliver(w, v, h, w_out, v_out, h_out, sem):
+    copies = [
+        pltpu.make_async_copy(src, dst, sem.at[i])
+        for i, (src, dst) in enumerate([(w, w_out), (v, v_out), (h, h_out)])
+    ]
+    for copy in copies:
+        copy.start()
+    for copy in copies:
+        copy.wait()
 
 
 def local(counts, shared, view_factors, loadings):
@@ -290,25 +335,33 @@
             vmem((RANK, cells)),
             vmem((LANES, LANES)),
             vmem((CHIPS, RANK, LANES)),
-            vmem((8, LANES)),
+            vmem((2, 4, LANES)),
             vmem((DEVICES, ROWS, LANES)),
-            vmem((DEVICES, 8, LANES)),
+            vmem((DEVICES, 4, LANES)),
             pltpu.VMEM((LANES, 2 * LANES), bf16),
-            vmem((ROWS, LANES)),
-            vmem((8, LANES)),
+            pltpu.VMEM((RANK, LANES), bf16),
+            vmem((RANK, LANES)),
             vmem((2, 2, HALF, LANES)),
             vmem((2, HALF, LANES)),
             vmem((2, HALF, LANES)),
-            vmem((OUTER_STEPS, SETS // 2, 2, HALF, LANES)),
-            vmem((RANK, LANES)),
+            vmem((OUTER_STEPS, 2, SETS // 2, HALF, LANES)),
+            vmem((2 * DEVICES - 1, HALF, LANES)),
             dma((CHIPS,)), dma((3,)), dma((3,)),
-            dma, dma, dma, dma, dma, dma((GROUPS,)),
-            dma, dma, dma((OUTER_STEPS,)), dma((OUTER_STEPS,)), dma, dma, dma, dma,
+            dma, dma, dma, dma, dma, dma((CHIPS,)),
+            dma((2,)), dma((2,)), dma((OUTER_STEPS, 2)), dma((OUTER_STEPS, 2)), dma, dma,
+            pltpu.SemaphoreType.REGULAR((2,)),
         ],
         compiler_params=pltpu.CompilerParams(
-            collective_id=0, has_side_effects=True, vmem_limit_bytes=40 * 2**20
+            collective_id=0, has_side_effects=True, vmem_limit_bytes=60 * 2**20
         ),
     )(counts[0], shared, view_factors[0], loadings[0])
+    w, v, h = pl.pallas_call(
+        deliver,
+        out_shape=[jax.ShapeDtypeStruct(a.shape, f32) for a in (w, v, h)],
+        in_specs=[pl.BlockSpec(memory_space=pltpu.VMEM)] * 3,
+        out_specs=[hbm] * 3,
+        scratch_shapes=[dma((3,))],
+    )(w, v, h)
     return w, v[None], h[None]
 
 

time: 142 us -> 128 us (0.901)
  local copies, waits for them, and re-layouts: 7.05 us -> 0 us
  Pallas kernels: 134 us -> 127 us
    pallas_call x1, Pallas kernels: 134 us -> 125 us  [local(): pl.pallas_call(kernel, out_shape=[jax.ShapeDtypeStruct((RANK, genes), f32...]
    unnamed x11 -> x0, local copies, waits for them, and re-layouts: 7.05 us -> none
    pallas_call x0 -> x1, Pallas kernels: none -> 1.92 us  [local(): pl.pallas_call(deliver, out_shape=[jax.ShapeDtypeStruct(a.shape, f32) for...]
where the time goes in v2:
time: 128 us
  Pallas kernels  127 us (99%)
    pallas_call x1, Pallas kernels, local(): pl.pallas_call(kernel, out_shape=[jax.ShapeDtypeStruct((RANK, genes), f32...  125 us

profile of v2, /device:TPU:1, one launch (start us, length us, event | category | flops | bytes accessed | tf_op | source)
XLA Modules:
  0.0 127.9 jit_solution(17211545123578841229)
XLA Ops:
  0.6 125.4 %shard_map.67 = (f32[32,2048]{1,0:T(8,128)}, f32[32,2048]{1,0:T(8,128)}, f32[32,1024]{1,0:T(8,128)}) custom-call(bf16[2048,1024]{1,0:T(8,128)(2,1)} %bitcast.5, f32[32,2048]{1,0:T(8,128)} %w_hbm.1, f32[32,2048]{1,0:T(8,128)} %bitcast.6, f32[32,1024]{1,0:T(8,128)} %bitcast.7), custom_call_target="tpu_custom_call" | custom-call | tf_op jit(solution)/shard_map/pallas_call | solution.py:321
  126.0 1.9 %shard_map.68 = (f32[32,2048]{1,0:T(8,128)}, f32[32,2048]{1,0:T(8,128)}, f32[32,1024]{1,0:T(8,128)}) custom-call(f32[32,2048]{1,0:T(8,128)} %get-tuple-element.9.w, f32[32,2048]{1,0:T(8,128)} %get-tuple-element.10.v, f32[32,1024]{1,0:T(8,128)} %get-tuple-element.11.h), custom_call_target="tpu_custom_call" | custom-call | tf_op jit(solution)/shard_map/pallas_call | solution.py:358

commit v3 on v2

--- a/solution.py
+++ b/solution.py
@@ -24,6 +24,7 @@
 MESH = pl.DeviceIdType.MESH
 NN = (((1,), (0,)), ((), ()))
 NT = (((1,), (1,)), ((), ()))
+TN = (((0,), (0,)), ((), ()))
 
 
 def hops(d):
@@ -48,8 +49,8 @@
 
 def kernel(
     x_hbm, w_hbm, v_hbm, h_hbm, w_out, v_out, h_out,
-    x, w, v, h, n, z, parts, qsrc, pslots, qslots, m4, qleft, wold,
-    zsrc, zpair, zhalf, zslots, blank,
+    x, w, v, h, n, z, parts, qsrc, pslots, qslots, m4, qleft,
+    psrc, ppair, dsrc, dslots, zhalf, zslots, blank,
     xsem, insem, outsem, psend, precv, qsend, qrecv, vsend, vrecv,
     z1send, z1recv, z2send, z2recv, wsend, wrecv, hand,
 ):
@@ -109,29 +110,33 @@
     pltpu.make_async_copy(w, w, insem.at[0]).wait()
     pltpu.make_async_copy(v, v, insem.at[1]).wait()
 
-    def gather(i, c, first):
-        vc = v[c]
-        a = w[c] + vc
-        ah, al = split(a)
-        vh, vl = split(vc)
-        s = jnp.concatenate([ah, al, vh, vl], axis=0)
-        rows = pl.ds(pl.multiple_of(c * LANES, LANES), LANES)
-        dn, dz = dot(ah, x[rows, :]), dot(s, s, NT)
-        if first:
+    def gather(batch):
+        dn, dz, held = 0, 0, []
+        for i in batch:
+            c = chips[i]
+            vc = v[c]
+            a = w[c] + vc
+            ah, al = split(a)
+            vh, vl = split(vc)
+            held.append(jnp.concatenate([ah, al, vh, vl], axis=0))
+            rows = pl.ds(pl.multiple_of(c * LANES, LANES), LANES)
+            dn = dn + dot(ah, x[rows, :])
+        for j in range(0, len(held), 2):
+            s = jnp.concatenate(held[j : j + 2], axis=1)
+            dz = dz + dot(s, s, NT)
+        if batch[0] == 0:
             n[...] = dn
             z[...] = dz
         else:
             n[...] += dn
             z[...] += dz
 
-    for i in range(CHIPS):
-        load_x(i).wait()
-        gather(i, chips[i], i == 0)
+    groups = [range(0, 5), range(5, 11), range(11, 16)]
+    for batch in groups:
+        for i in batch:
+            load_x(i).wait()
+        gather(batch)
     load_h().wait()
-    pl.semaphore_wait(barrier, count)
-
-    for where in (along(-2), along(2), {"dp": pair}):
-        pl.semaphore_signal(hand.at[0], inc=1, device_id=where, device_id_type=MESH)
 
     lane = lax.broadcasted_iota(jnp.int32, (RANK, LANES), 1)
     row = lax.broadcasted_iota(jnp.int32, (RANK, LANES), 0)
@@ -155,6 +160,9 @@
 
     def wait_v(i):
         settle(pslots.at[pl.ds(0, 2 if i else 1)], vsend, vrecv.at[i]).wait_recv()
+
+    def wait_w(i):
+        settle(blank.at[pl.ds(0, 4 if i else 3)], wsend, wrecv.at[i]).wait_recv()
 
     def step(t, carry):
         zz = z[...]
@@ -169,32 +177,39 @@
         h[...] = hv
         hh, hl = split(hv)
 
-        two = jnp.concatenate([hh, hl], axis=0)
-        q = dot(two, jnp.concatenate([two, two], axis=0), NT)
-        q = q[:32] + q[32:]
-        q = q + pltpu.roll(q, 32, 1)
-        q = jnp.where(block == lax.rem(row // 4, 4), q, 0.0)
-        for k in range(2):
-            packed = q[ROWS * k : ROWS * k + 8] + q[ROWS * k + 8 : ROWS * k + 16]
-            packed = packed + pltpu.roll(packed, 4, 0)
-            qsrc[k] = packed[:4]
-        qslots[me] = qsrc[core]
-        for i in reversed(range(CHIPS)):
-            for c, k in partners(i):
-                remote(qsrc.at[k], qslots.at[me], qsend, qrecv, {"cell": c * 2 + k}).start()
-
         old = v[chip]
-        shared = w[chip]
-        wold[...] = shared
-        m4[...] = spread(shared + old + PENALTY * old)
-
-        for i in reversed(range(CHIPS)):
-            c = chips[i]
-            rows = pl.ds(pl.multiple_of(c * LANES, LANES), LANES)
-            parts[c] = dot(hh, x[rows, :], NT)
-            for c, k in partners(i):
-                its = pl.ds(pl.multiple_of(k * ROWS, ROWS), ROWS)
-                remote(parts.at[c, its], pslots.at[me], psend, precv, {"cell": c * 2 + k}).start()
+        m4[...] = spread(w[chip] + old + PENALTY * old)
+
+        for batch in reversed(groups):
+            for i in reversed(batch):
+                rows = pl.ds(pl.multiple_of(chips[i] * LANES, LANES), LANES)
+                parts[chips[i]] = dot(hh, x[rows, :], NT)
+            if batch is groups[-1]:
+
+                @pl.when(t < 1)
+                def _():
+                    pl.semaphore_wait(barrier, count)
+                    for where in (along(-2), along(2), {"dp": pair}):
+                        pl.semaphore_signal(hand.at[0], inc=1, device_id=where, device_id_type=MESH)
+
+            for i in reversed(batch):
+                for c, k in partners(i):
+                    its = pl.ds(pl.multiple_of(k * ROWS, ROWS), ROWS)
+                    remote(parts.at[c, its], pslots.at[me], psend, precv, {"cell": c * 2 + k}).start()
+            if batch is groups[-1]:
+                two = jnp.concatenate([hh, hl], axis=0)
+                q = dot(two, jnp.concatenate([two, two], axis=0), NT)
+                q = q[:32] + q[32:]
+                q = q + pltpu.roll(q, 32, 1)
+                q = jnp.where(block == lax.rem(row // 4, 4), q, 0.0)
+                for k in range(2):
+                    packed = q[ROWS * k : ROWS * k + 8] + q[ROWS * k + 8 : ROWS * k + 16]
+                    packed = packed + pltpu.roll(packed, 4, 0)
+                    qsrc[k] = packed[:4]
+                qslots[me] = qsrc[core]
+                for i in reversed(range(CHIPS)):
+                    for c, k in partners(i):
+                        remote(qsrc.at[k], qslots.at[me], qsend, qrecv, {"cell": c * 2 + k}).start()
         pslots[me] = parts[chip, mine]
 
         settle(qslots.at[pl.ds(0, DEVICES - 1)], qsend, qrecv).wait()
@@ -218,17 +233,10 @@
             for s in (-4, 4):
                 pl.semaphore_signal(hand.at[1], inc=1, device_id=along(s), device_id_type=MESH)
 
-        def to_pair(j):
-            return remote(zsrc.at[j, 1 - parity], zpair.at[j], z1send.at[j], z1recv.at[j], {"dp": pair})
-
-        def halve(j, total):
-            zsrc[j, 0] = total[:HALF]
-            zsrc[j, 1] = total[HALF:]
-            to_pair(j).start()
-
-        def to_others(j):
-            to_pair(j).wait()
-            half = zsrc[j, parity] + zpair[j]
+        def first_half():
+            return remote(psrc.at[1 - parity], ppair, z1send.at[0], z1recv.at[0], {"dp": pair})
+
+        def to_others(j, half):
             zhalf[j] = half
             spot = lax.div(dp, 2)
             zslots[turn, j, spot] = half
@@ -246,27 +254,42 @@
 
         @pl.when(last)
         def _():
-            halve(0, pt)
+            psrc[0] = pt[:HALF]
+            psrc[1] = pt[HALF:]
+            first_half().start()
 
         v[chip, mine] = v[chip, mine] * pt / d
         to_all(v.at[chip, mine], vsend, vrecv)
-        wait_v(0)
 
         @pl.when(last)
         def _():
-            halve(1, square_times(qleft[...], spread(wold[...] + v[chip])))
+            high, low = split(w[chip, mine] + v[chip, mine])
+            e = dot(jnp.concatenate([qleft[...]] * 2, axis=0), jnp.concatenate([high, high, low, low], axis=0), TN)
+            e = (e[:32] + e[32:64]) + (e[64:96] + e[96:])
+            for k in range(2):
+                for p in range(2):
+                    dsrc[k, p] = e[ROWS * k + HALF * p : ROWS * k + HALF * (p + 1)]
+            other = chip * 2 + 1 - core
+            for spot, (k, p, where) in enumerate([
+                (1 - core, 1 - parity, {"dp": pair, "cell": other}),
+                (core, 1 - parity, {"dp": pair}),
+                (1 - core, parity, {"cell": other}),
+            ]):
+                remote(dsrc.at[k, p], dslots.at[spot], z1send.at[1], z1recv.at[1], where).start()
 
             @pl.when(turn == 0)
             def _():
                 pl.semaphore_wait(hand.at[1], 2)
 
-            to_others(0)
-            to_others(1)
+            first_half().wait()
+            to_others(0, psrc[parity] + ppair[...])
+            settle(dslots, z1send.at[1], z1recv.at[1]).wait()
+            to_others(1, (dsrc[core, parity] + dslots[0]) + (dslots[1] + dslots[2]))
 
             @pl.when(turn == OUTER_STEPS - 1)
             def _():
                 pltpu.make_async_copy(h, h_out, outsem.at[0]).start()
-                for i in range(1, CHIPS):
+                for i in range(CHIPS):
                     wait_v(i)
                 for c in range(CHIPS):
                     pltpu.make_async_copy(v.at[c], v_out.at[:, pl.ds(c * LANES, LANES)], outsem.at[1]).start()
@@ -280,17 +303,33 @@
                 for z_to in (pair, dp):
                     for k in (1 - core, core):
                         if i or z_to is pair or k is not core:
-                            remote(piece, piece, wsend, wrecv, {"dp": z_to, "cell": chips[i] * 2 + k}).start()
-            settle(blank, wsend, wrecv).wait()
+                            where = {"dp": z_to, "cell": chips[i] * 2 + k}
+                            remote(piece, piece, wsend, wrecv.at[MIRROR[i]], where).start()
+
+            @pl.when(turn == OUTER_STEPS - 1)
+            def _():
+                for i in range(CHIPS):
+                    wait_w(i)
 
         @pl.when(t < ITERS * OUTER_STEPS - 1)
         def _():
-            for i in range(CHIPS):
-                if i:
+            for batch in groups:
+                for i in batch:
                     wait_v(i)
-                gather(i, chips[i], i == 0)
+
+                @pl.when(last)
+                def _():
+                    for i in batch:
+                        wait_w(i)
+
+                gather(batch)
 
         settle(pslots.at[pl.ds(0, DEVICES - 1)], vsend, vrecv.at[0]).wait_send()
+
+        @pl.when(last)
+        def _():
+            settle(blank, wsend, wrecv.at[0]).wait_send()
+
         return carry
 
     lax.fori_loop(0, ITERS * OUTER_STEPS, step, 0)
@@ -340,15 +379,16 @@
             vmem((DEVICES, 4, LANES)),
             pltpu.VMEM((LANES, 2 * LANES), bf16),
             pltpu.VMEM((RANK, LANES), bf16),
-            vmem((RANK, LANES)),
+            vmem((2, HALF, LANES)),
+            vmem((HALF, LANES)),
             vmem((2, 2, HALF, LANES)),
-            vmem((2, HALF, LANES)),
+            vmem((3, HALF, LANES)),
             vmem((2, HALF, LANES)),
             vmem((OUTER_STEPS, 2, SETS // 2, HALF, LANES)),
             vmem((2 * DEVICES - 1, HALF, LANES)),
             dma((CHIPS,)), dma((3,)), dma((3,)),
             dma, dma, dma, dma, dma, dma((CHIPS,)),
-            dma((2,)), dma((2,)), dma((OUTER_STEPS, 2)), dma((OUTER_STEPS, 2)), dma, dma,
+            dma((2,)), dma((2,)), dma((OUTER_STEPS, 2)), dma((OUTER_STEPS, 2)), dma, dma((CHIPS,)),
             pltpu.SemaphoreType.REGULAR((2,)),
         ],
         compiler_params=pltpu.CompilerParams(

time: 128 us -> 121 us (0.945)
  Pallas kernels: 127 us -> 120 us
    pallas_call x1, Pallas kernels: 125 us -> 118 us  [local(): pl.pallas_call(kernel, out_shape=[jax.ShapeDtypeStruct((RANK, genes), f32...]
where the time goes in v3:
time: 121 us
  Pallas kernels  120 us (99%)
    pallas_call x1, Pallas kernels, local(): pl.pallas_call(kernel, out_shape=[jax.ShapeDtypeStruct((RANK, genes), f32...  118 us

profile of v3, /device:TPU:1, one launch (start us, length us, event | category | flops | bytes accessed | tf_op | source)
XLA Modules:
  0.0 120.9 jit_solution(1521243940787090204)
XLA Ops:
  0.6 118.4 %shard_map.67 = (f32[32,2048]{1,0:T(8,128)}, f32[32,2048]{1,0:T(8,128)}, f32[32,1024]{1,0:T(8,128)}) custom-call(bf16[2048,1024]{1,0:T(8,128)(2,1)} %bitcast.5, f32[32,2048]{1,0:T(8,128)} %w_hbm.1, f32[32,2048]{1,0:T(8,128)} %bitcast.6, f32[32,1024]{1,0:T(8,128)} %bitcast.7), custom_call_target="tpu_custom_call" | custom-call | tf_op jit(solution)/shard_map/pallas_call | solution.py:360
  119.0 1.9 %shard_map.68 = (f32[32,2048]{1,0:T(8,128)}, f32[32,2048]{1,0:T(8,128)}, f32[32,1024]{1,0:T(8,128)}) custom-call(f32[32,2048]{1,0:T(8,128)} %get-tuple-element.9.w, f32[32,2048]{1,0:T(8,128)} %get-tuple-element.10.v, f32[32,1024]{1,0:T(8,128)} %get-tuple-element.11.h), custom_call_target="tpu_custom_call" | custom-call | tf_op jit(solution)/shard_map/pallas_call | solution.py:398

commit v4 on v3

--- a/solution.py
+++ b/solution.py
@@ -189,11 +189,14 @@
                 @pl.when(t < 1)
                 def _():
                     pl.semaphore_wait(barrier, count)
-                    for where in (along(-2), along(2), {"dp": pair}):
+                    for where in (along(-2), along(-1), along(1), along(2)):
                         pl.semaphore_signal(hand.at[0], inc=1, device_id=where, device_id_type=MESH)
 
-            for i in reversed(batch):
-                for c, k in partners(i):
+            for other in (1, 0):
+                for i in reversed(batch):
+                    if not (other or i):
+                        continue
+                    c, k = chips[i], 1 - core if other else core
                     its = pl.ds(pl.multiple_of(k * ROWS, ROWS), ROWS)
                     remote(parts.at[c, its], pslots.at[me], psend, precv, {"cell": c * 2 + k}).start()
             if batch is groups[-1]:
@@ -207,8 +210,8 @@
                     packed = packed + pltpu.roll(packed, 4, 0)
                     qsrc[k] = packed[:4]
                 qslots[me] = qsrc[core]
-                for i in reversed(range(CHIPS)):
-                    for c, k in partners(i):
+                for i, other in [(i, other) for other in (1, 0) for i in reversed(range(CHIPS)) if i or other]:
+                    for c, k in [(chips[i], 1 - core if other else core)]:
                         remote(qsrc.at[k], qslots.at[me], qsend, qrecv, {"cell": c * 2 + k}).start()
         pslots[me] = parts[chip, mine]
 
@@ -219,19 +222,14 @@
         qt = jnp.where(block[:ROWS] == row[:ROWS] // 4, jnp.concatenate([qt] * 4, axis=0), 0.0)
         left = jnp.concatenate(split(qt), axis=0)
         qleft[...] = left
-        d = square_times(left, m4[...])
+        ratio = v[chip, mine] / square_times(left, m4[...])
         settle(pslots.at[pl.ds(0, DEVICES - 1)], psend, precv).wait()
-        pt = pslots[0]
-        for i in range(1, DEVICES):
-            pt = pt + pslots[i]
+        pt = [pslots[i] for i in range(DEVICES)]
+        while len(pt) > 1:
+            pt = [a + b for a, b in zip(pt[::2], pt[1::2])]
+        pt = pt[0]
         turn = lax.div(t, ITERS)
         last = lax.rem(t, ITERS) == ITERS - 1
-
-        @pl.when(t == 0)
-        def _():
-            pl.semaphore_wait(hand.at[0], 3)
-            for s in (-4, 4):
-                pl.semaphore_signal(hand.at[1], inc=1, device_id=along(s), device_id_type=MESH)
 
         def first_half():
             return remote(psrc.at[1 - parity], ppair, z1send.at[0], z1recv.at[0], {"dp": pair})
@@ -252,17 +250,20 @@
                 total = total + zslots[turn, j, i]
             return total
 
+        v[chip, mine] = pt * ratio
+        to_all(v.at[chip, mine], vsend, vrecv)
+        psrc[0] = pt[:HALF]
+        psrc[1] = pt[HALF:]
+
+        @pl.when(t == 0)
+        def _():
+            pl.semaphore_wait(hand.at[0], 4)
+            for s in (-4, 4):
+                pl.semaphore_signal(hand.at[1], inc=1, device_id=along(s), device_id_type=MESH)
+
         @pl.when(last)
         def _():
-            psrc[0] = pt[:HALF]
-            psrc[1] = pt[HALF:]
             first_half().start()
-
-        v[chip, mine] = v[chip, mine] * pt / d
-        to_all(v.at[chip, mine], vsend, vrecv)
-
-        @pl.when(last)
-        def _():
             high, low = split(w[chip, mine] + v[chip, mine])
             e = dot(jnp.concatenate([qleft[...]] * 2, axis=0), jnp.concatenate([high, high, low, low], axis=0), TN)
             e = (e[:32] + e[32:64]) + (e[64:96] + e[96:])
@@ -300,20 +301,21 @@
             w[chip, ours] = w[chip, ours] * numerator / denominator
             piece = w.at[chip, ours]
             for i in reversed(range(CHIPS)):
-                for z_to in (pair, dp):
-                    for k in (1 - core, core):
-                        if i or z_to is pair or k is not core:
-                            where = {"dp": z_to, "cell": chips[i] * 2 + k}
-                            remote(piece, piece, wsend, wrecv.at[MIRROR[i]], where).start()
+                for z_to, k in ((along(1), core), (along(-1), 1 - core), ({}, 1 - core), ({}, core)):
+                    if i or z_to or k is not core:
+                        where = {"cell": chips[i] * 2 + k, **z_to}
+                        remote(piece, piece, wsend, wrecv.at[MIRROR[i]], where).start()
 
             @pl.when(turn == OUTER_STEPS - 1)
             def _():
                 for i in range(CHIPS):
                     wait_w(i)
+                    genes = pl.ds(pl.multiple_of(chips[i] * LANES, LANES), LANES)
+                    pltpu.make_async_copy(w.at[chips[i]], w_out.at[:, genes], outsem.at[2]).start()
 
         @pl.when(t < ITERS * OUTER_STEPS - 1)
         def _():
-            for batch in groups:
+            for batch in (groups[0], groups[2], groups[1]):
                 for i in batch:
                     wait_v(i)
 
@@ -334,8 +336,6 @@
 
     lax.fori_loop(0, ITERS * OUTER_STEPS, step, 0)
 
-    for c in range(CHIPS):
-        pltpu.make_async_copy(w.at[c], w_out.at[:, pl.ds(c * LANES, LANES)], outsem.at[2]).start()
     pltpu.make_async_copy(h, h_out, outsem.at[0]).wait()
     pltpu.make_async_copy(v, v, outsem.at[1]).wait()
     pltpu.make_async_copy(w, w, outsem.at[2]).wait()

time: 121 us -> 120 us (level)
  no operation moved by 1% of the time
where the time goes in v4:
time: 120 us
  Pallas kernels  119 us (99%)
    pallas_call x1, Pallas kernels, local(): pl.pallas_call(kernel, out_shape=[jax.ShapeDtypeStruct((RANK, genes), f32...  117 us

profile of v4, /device:TPU:1, one launch (start us, length us, event | category | flops | bytes accessed | tf_op | source)
XLA Modules:
  0.0 119.8 jit_solution(10721149203400231308)
XLA Ops:
  0.6 117.2 %shard_map.67 = (f32[32,2048]{1,0:T(8,128)}, f32[32,2048]{1,0:T(8,128)}, f32[32,1024]{1,0:T(8,128)}) custom-call(bf16[2048,1024]{1,0:T(8,128)(2,1)} %bitcast.5, f32[32,2048]{1,0:T(8,128)} %w_hbm.1, f32[32,2048]{1,0:T(8,128)} %bitcast.6, f32[32,1024]{1,0:T(8,128)} %bitcast.7), custom_call_target="tpu_custom_call" | custom-call | tf_op jit(solution)/shard_map/pallas_call | solution.py:360
  117.9 1.9 %shard_map.68 = (f32[32,2048]{1,0:T(8,128)}, f32[32,2048]{1,0:T(8,128)}, f32[32,1024]{1,0:T(8,128)}) custom-call(f32[32,2048]{1,0:T(8,128)} %get-tuple-element.9.w, f32[32,2048]{1,0:T(8,128)} %get-tuple-element.10.v, f32[32,1024]{1,0:T(8,128)} %get-tuple-element.11.h), custom_call_target="tpu_custom_call" | custom-call | tf_op jit(solution)/shard_map/pallas_call | solution.py:398
